TPU v7x, 32 devices: a whole 2x2x4 slice. The times are simulated.
32 devices in a mesh: groups: 2 (over y), tensor: 4 (over z), dp: 4 (over x, core).
Axes of the slice: x: 2, y: 2, z: 4, core: 2. Of those that a mesh axis runs over, the one named last changes fastest.
Arguments:
- attention: bfloat16 [3, 2048, 8192], P(None, ('groups', 'dp'), 'tensor'), parts along dimension 1, may hold values from -6 to 6
- out_proj: bfloat16 [3, 8192, 8192], P(None, 'tensor', 'dp'), may hold values from -0.0625 to 0.0625
- join_weight: bfloat16 [3, 8192, 8192], P(None, 'dp', 'tensor'), may hold values from -0.0390625 to 0.0390625
- cotangent: bfloat16 [2048, 8192], P(('groups', 'dp'), 'tensor'), parts along dimension 0, may hold values from -0.1875 to 0.1875
- loss_mask: int32 [2048], P(('groups', 'dp')), parts along dimension 0, may hold values 0 or 1
Outputs:
- joined_out: bfloat16 [2048, 8192], P(('groups', 'dp'), 'tensor'), parts along dimension 0
- gradient: bfloat16 [6, 8192, 8192], P('groups', 'dp', 'tensor'), parts along dimension 0
There are 2 independent parts, one for each index of `groups`. A program takes and returns all parts, laid end to end along the dimension named above; an argument that names none is the same for every part. Nothing has to cross between parts.
All inputs are finite; a program needn't handle non-finite values. No bound on the sum of `loss_mask` on one device may be relied on, other than what follows from the above.
Results may differ from a plain program's by a relative error of at most 0.015.
Values may be sent and summed in bfloat16 or wider, within the bound.
No kernel may reach another device: no remote copies, remote signals or barrier semaphores. Data moves between devices by JAX's collectives and lax.ppermute only.
A program may use at most 256 MiB of HBM per device.

v0:
```python
import jax
import jax.numpy as jnp
from jax import lax
from jax.sharding import PartitionSpec as P


def shards(attention, out_proj, join_weight, cotangent, loss_mask):
    partial_value = jnp.einsum(
        "lrk,lkc->rlc",
        lax.all_gather(attention, "dp", axis=1, tiled=True),
        out_proj,
        preferred_element_type=jnp.float32,
    )
    masked = cotangent * loss_mask[:, None].astype(jnp.bfloat16)
    cotangent_all = lax.all_gather(masked, "dp", axis=0, tiled=True)
    summed = lax.psum(partial_value.astype(jnp.bfloat16), "tensor")
    joined_part = jnp.einsum("rlf,lfc->rc", summed, join_weight, preferred_element_type=jnp.float32)
    gradient = jnp.einsum("rlf,rc->lfc", summed, cotangent_all, preferred_element_type=jnp.float32)
    joined_out = lax.psum_scatter(
        joined_part.astype(jnp.bfloat16), "dp", scatter_dimension=0, tiled=True
    )
    return (joined_out, gradient.astype(jnp.bfloat16))


def solution(mesh):
    placed = (
        P(None, ("groups", "dp"), "tensor"),
        P(None, "tensor", "dp"),
        P(None, "dp", "tensor"),
        P(("groups", "dp"), "tensor"),
        P(("groups", "dp")),
    )
    return jax.shard_map(
        shards,
        mesh=mesh,
        in_specs=placed,
        out_specs=(P(("groups", "dp"), "tensor"), P("groups", "dp", "tensor")),
        check_vma=False,
    )
```

profile of v0, /device:TPU:0, one launch (start us, length us, event | category | flops | bytes accessed | tf_op | source)
XLA Modules:
  0.0 648.6 jit_solution(13141308082697358008)
XLA Ops:
  7.2 0.0 all-gather.3.cloned.1.call-start
  7.2 0.7 all-gather.3.cloned.1.call-update
  7.9 0.0 all-reduce.2.cloned.1.call-start
  7.9 86.5 %all-gather.3.cloned.1.call-done = bf16[3,1024,2048]{2,1,0:T(8,128)(2,1)} async-done(((bf16[3,256,2048]{2,1,0:T(8,128)(2,1)}), bf16[3,1024,2048]{2,1,0:T(8,128)(2,1)}) %all-gather.3.cloned.1.call-update) | async-done | bytes 12582928 | tf_op jit(solution)/shard_map/all_gather | solution.py:10
  94.4 38.8 %convert_bitcast_fusion = bf16[1024,3,2048]{0,2,1:T(8,128)(2,1)} fusion(bf16[3,2048,2048]{2,1,0:T(8,128)(2,1)} %param.6, bf16[3,1024,2048]{2,1,0:T(8,128)(2,1)} %all-gather.3.cloned.1.call-done), kind=kOutput, calls=%fused_computation.1 | convolution fusion | flops 25776095232 | bytes 50331648 | tf_op jit(solution)/shard_map/lrk,lkc->rlc/dot_general | solution.py:8
  133.2 0.0 copy-start.1
  133.2 0.0 copy-start
  133.2 0.0 all-reduce.2.cloned.1.call-update
  133.3 0.0 all-gather.5.cloned.1.call-start
  133.3 0.6 copy-done.1
  133.9 0.6 copy-done
  134.5 1.1 broadcast_multiply_fusion
  135.6 0.0 all-gather.5.cloned.1.call-update
  135.6 0.0 reduce-scatter.2.cloned.1.call-start
  135.6 423.9 %all-reduce.2.cloned.1.call-done = bf16[1024,3,2048]{0,2,1:T(8,128)(2,1)} async-done(((bf16[1024,3,2048]{0,2,1:T(8,128)(2,1)}), bf16[1024,3,2048]{0,2,1:T(8,128)(2,1)}) %all-reduce.2.cloned.1.call-update) | async-done | bytes 12582928 | tf_op jit(solution)/shard_map/psum | solution.py:16
  559.5 34.2 %bitcast_convert_fusion = bf16[1024,2048]{1,0:T(8,128)(2,1)} fusion(bf16[1024,3,2048]{0,2,1:T(8,128)(2,1)} %all-reduce.2.cloned.1.call-done, bf16[3,2048,2048]{2,1,0:T(8,128)(2,1)} %param.7), kind=kOutput, calls=%fused_computation.2 | convolution fusion | flops 25771900928 | bytes 41943040 | tf_op jit(solution)/shard_map/rlf,lfc->rc/dot_general | solution.py:17
  593.8 0.0 reduce-scatter.2.cloned.1.call-update
  593.8 0.8 all-gather.5.cloned.1.call-done
  594.6 33.6 %convolution_convert_fusion = bf16[3,2048,2048]{2,1,0:T(8,128)(2,1)} fusion(bf16[1024,3,2048]{0,2,1:T(8,128)(2,1)} %all-reduce.2.cloned.1.call-done, bf16[1024,2048]{1,0:T(8,128)(2,1)} %all-gather.5.cloned.1.call-done), kind=kOutput, calls=%fused_computation | convolution fusion | flops 25782386688 | bytes 41943040 | tf_op jit(solution)/shard_map/rlf,rc->lfc/dot_general | solution.py:18
  628.1 13.9 %reduce-scatter.2.cloned.1.call-done = bf16[256,2048]{1,0:T(8,128)(2,1)} async-done(((bf16[1024,2048]{1,0:T(8,128)(2,1)}), bf16[256,2048]{1,0:T(8,128)(2,1)}) %reduce-scatter.2.cloned.1.call-update) | async-done | bytes 1048592 | tf_op jit(solution)/shard_map/reduce_scatter | solution.py:19
  (1 shorter events, 0.0 us)
Async XLA Ops:
  7.2 87.2 %all-gather.3.cloned.1.call-start = ((), (), s32[]{:S(2)}) async-start(), calls=%async_computation.1 | async-start | bytes 15728640 | tf_op jit(solution)/shard_map/all_gather | solution.py:10
  7.9 551.6 %all-reduce.2.cloned.1.call-start = ((), (), s32[]{:S(2)}) async-start(), calls=%async_computation.2 | async-start | bytes 25165824 | tf_op jit(solution)/shard_map/psum | solution.py:16
  133.2 0.7 copy-start.1
  133.2 1.2 copy-start
  133.3 461.3 %all-gather.5.cloned.1.call-start = ((), (), s32[]{:S(2)}) async-start(), calls=%async_computation.4 | async-start | bytes 5242880 | tf_op jit(solution)/shard_map/all_gather | solution.py:15
  135.6 506.4 %reduce-scatter.2.cloned.1.call-start = ((), (), s32[]{:S(2)}) async-start(), calls=%async_computation.3 | async-start | bytes 5242880 | tf_op jit(solution)/shard_map/reduce_scatter | solution.py:19
Sparse Core Ops, SparseCore 0:
  9.6 84.7 all-gather.2
  133.4 426.1 all-reduce.1
  561.1 33.4 all-gather.4
  597.5 44.4 reduce-scatter.1
where the time goes:
time: 649 us
  waiting for transfers between devices  526 us (81%)
  matrix products  107 us (16%)
  between operations  13.8 us (2%)
    psum x1, waiting for transfers between devices, shards(): summed = lax.psum(partial_value.astype(jnp.bfloat16), 'tensor')  424 us
    all_gather x1, waiting for transfers between devices, shards(): lax.all_gather(attention, 'dp', axis=1, tiled=True)  86.5 us
    dot_general x1, matrix products, shards(): jnp.einsum('lrk,lkc->rlc', lax.all_gather(attention, 'dp', axis=1, tiled=...  38.8 us
    dot_general x1, matrix products, shards(): jnp.einsum('rlf,lfc->rc', summed, join_weight, preferred_element_type=jnp...  34.2 us
    dot_general x1, matrix products, shards(): jnp.einsum('rlf,rc->lfc', summed, cotangent_all, preferred_element_type=j...  33.6 us
    reduce_scatter x1, waiting for transfers between devices, shards(): lax.psum_scatter(joined_part.astype(jnp.bfloat16), 'dp', scatter_dimensio...  13.9 us
  transfers between devices with their start and end apart: 4, of which 4 were waited for; matrix products, arithmetic and copies ran while one was open for 11% of the time, Pallas kernels for 0%

commit v1 on v0

v1 whole, which is shorter than its diff:
```python
import jax
import jax.numpy as jnp
from jax import lax
from jax.sharding import PartitionSpec as P

F32 = jnp.float32
BF16 = jnp.bfloat16


def plain(attention, out_proj, join_weight, cotangent, loss_mask):
    partial_value = jnp.einsum(
        "lrk,lkc->rlc",
        lax.all_gather(attention, "dp", axis=1, tiled=True),
        out_proj,
        preferred_element_type=F32,
    )
    masked = cotangent * loss_mask[:, None].astype(BF16)
    cotangent_all = lax.all_gather(masked, "dp", axis=0, tiled=True)
    summed = lax.psum(partial_value.astype(BF16), "tensor")
    joined_part = jnp.einsum("rlf,lfc->rc", summed, join_weight, preferred_element_type=F32)
    gradient = jnp.einsum("rlf,rc->lfc", summed, cotangent_all, preferred_element_type=F32)
    joined_out = lax.psum_scatter(joined_part.astype(BF16), "dp", scatter_dimension=0, tiled=True)
    return (joined_out, gradient.astype(BF16))


def dot(a, b):
    return jnp.dot(a, b, preferred_element_type=F32)


def chain(piece, n):
    total = piece.astype(F32)
    for hops in (
        [(s, s + 1) for s in range(n - 1)],
        [(s + 1, s) for s in reversed(range(n - 1))],
    ):
        send = piece
        for hop in hops:
            got = lax.ppermute(send, "tensor", [hop]).astype(F32)
            send = (piece.astype(F32) + got).astype(BF16)
            total = total + got
    return total.astype(BF16)


def chained(n, cuts):
    near = [(i, i ^ 1) for i in range(4)]
    far = [(i, i ^ 2) for i in range(4)]

    def gather(own):
        across = lax.ppermute(own, "dp", far)
        return [own, lax.ppermute(own, "dp", near), across, lax.ppermute(across, "dp", near)]

    def shards(attention, out_proj, join_weight, cotangent, loss_mask):
        layers, rows, _ = attention.shape
        step = rows // cuts
        masked = gather(cotangent * loss_mask[:, None].astype(BF16))
        joined = [None] * 4
        gradient = []
        for level in range(layers):
            last = level == layers - 1
            tokens = gather(attention[level])
            features = [None] * 4
            for j in (3, 2, 1, 0) if last else (0, 1, 2, 3):
                part = dot(tokens[j], out_proj[level]).astype(BF16)
                features[j] = jnp.concatenate(
                    [chain(part[q * step : (q + 1) * step], n) for q in range(cuts)], axis=0
                )
                term = dot(features[j], join_weight[level])
                joined[j] = term if joined[j] is None else joined[j] + term
            gradient.append(
                lax.dot_general(
                    jnp.concatenate(features, axis=0),
                    jnp.concatenate(masked, axis=0),
                    (((0,), (0,)), ((), ())),
                    preferred_element_type=F32,
                ).astype(BF16)
            )
        across = joined[2] + lax.ppermute(joined[3].astype(BF16), "dp", near).astype(F32)
        across = lax.ppermute(across.astype(BF16), "dp", far)
        beside = lax.ppermute(joined[1].astype(BF16), "dp", near)
        out = joined[0] + beside.astype(F32) + across.astype(F32)
        return (out.astype(BF16), jnp.stack(gradient, axis=0))

    return shards


def solution(mesh):
    placed = (
        P(None, ("groups", "dp"), "tensor"),
        P(None, "tensor", "dp"),
        P(None, "dp", "tensor"),
        P(("groups", "dp"), "tensor"),
        P(("groups", "dp")),
    )
    n = mesh.shape["tensor"]
    body = chained(n, 4) if mesh.shape["dp"] == 4 and n <= 8 else plain
    return jax.shard_map(
        body,
        mesh=mesh,
        in_specs=placed,
        out_specs=(P(("groups", "dp"), "tensor"), P("groups", "dp", "tensor")),
        check_vma=False,
    )
```

time: 649 us -> 1310 us (2.02); the launches traced: 649 us -> 1290 us
  starting transfers between devices: 0.16 us -> 326 us
  waiting for transfers between devices: 526 us -> 697 us
  matrix products: 107 us -> 187 us
  other arithmetic: 1.11 us -> 76.9 us
    ppermute x0 -> x303, waiting for transfers between devices: none -> 697 us  [the longest x288 677 us: chain(): got = lax.ppermute(send, 'tensor', [hop]).astype(F32)]
    psum x1 -> x0, waiting for transfers between devices: 424 us -> none  [shards(): summed = lax.psum(partial_value.astype(jnp.bfloat16), 'tensor')]
    ppermute x0 -> x303, starting transfers between devices: none -> 326 us  [the longest x288 319 us: chain(): got = lax.ppermute(send, 'tensor', [hop]).astype(F32)]
    all_gather x2 -> x0, waiting for transfers between devices: 87.2 us -> none  [the longest x1 86.5 us: shards(): lax.all_gather(attention, 'dp', axis=1, tiled=True)]
    dot_general x3 -> x27, matrix products: 107 us -> 187 us  [the longest x24 151 us: dot(): return jnp.dot(a, b, preferred_element_type=F32)]
    unnamed x0 -> x45, other arithmetic: none -> 42.7 us
    convert_element_type x1 -> x38, other arithmetic: 0.01 us -> 17.9 us  [the longest x36 16.4 us: chain(): send = (piece.astype(F32) + got).astype(BF16)]
    another operation x0 -> x1, other arithmetic: none -> 13.9 us  [shards(): return (out.astype(BF16), jnp.stack(gradient, axis=0))]
  transfers between devices with their start and end apart: 4 -> 303, of which waited for: 4 -> 72; matrix products, arithmetic and copies ran while one was open for 11% -> 20% of each run, Pallas kernels for 0% -> 0%
where the time goes in v1:
time: 1310 us; the launch traced here: 1290 us
  waiting for transfers between devices  697 us (53%)
  starting transfers between devices  326 us (25%)
  matrix products  187 us (14%)
  other arithmetic  76.9 us (6%)
    ppermute x288, waiting for transfers between devices, chain(): got = lax.ppermute(send, 'tensor', [hop]).astype(F32)  677 us
    ppermute x288, starting transfers between devices, chain(): got = lax.ppermute(send, 'tensor', [hop]).astype(F32)  319 us
    dot_general x24, matrix products, dot(): return jnp.dot(a, b, preferred_element_type=F32)  151 us
    unnamed x45, other arithmetic  42.7 us
    dot_general x3, matrix products, shards(): lax.dot_general(jnp.concatenate(features, axis=0), jnp.concatenate(masked...  36.6 us
  transfers between devices with their start and end apart: 303, of which 72 were waited for; matrix products, arithmetic and copies ran while one was open for 20% of the time, Pallas kernels for 0%

profile of v1, /device:TPU:0, one launch (start us, length us, event | category | flops | bytes accessed | tf_op | source)
XLA Modules:
  0.0 1294.1 jit_solution(12871479758677296553)
XLA Ops:
  0.6 6.2 fusion.114
  15.0 5.7 fusion.102
  20.8 5.8 fusion.126
  111.2 5.7 fusion.117
  117.0 8.7 collective-permute-done.173
  127.0 6.0 fusion.120
  133.7 5.7 fusion.105
  139.5 78.6 %collective-permute-done.29 = bf16[64,2048]{1,0:T(8,128)(2,1)S(1)} collective-permute-done((bf16[64,2048]{1,0:T(8,128)(2,1)S(1)}, bf16[64,2048]{1,0:T(8,128)(2,1)S(1)}, u32[]{:S(2)}, u32[]{:S(2)}) %collective-permute-start.29) | collective-permute-done | bytes 262176 | tf_op jit(solution)/shard_map/ppermute | solution.py:38
  221.1 10.8 collective-permute-done.35
  234.9 6.9 collective-permute-done.41
  244.7 6.0 collective-permute-done.47
  261.2 6.0 fusion.108
  287.5 5.8 fusion.72
  294.0 5.7 fusion.129
  314.7 7.1 fusion.84
  322.5 5.7 fusion.132
  490.4 206.9 %collective-permute-done.103 = bf16[64,2048]{1,0:T(8,128)(2,1)S(1)} collective-permute-done((bf16[64,2048]{1,0:T(8,128)(2,1)S(1)}, bf16[64,2048]{1,0:T(8,128)(2,1)S(1)}, u32[]{:S(2)}, u32[]{:S(2)}) %collective-permute-start.103) | collective-permute-done | bytes 262176 | tf_op jit(solution)/shard_map/ppermute | solution.py:38
  725.7 6.3 collective-permute-done.179
  734.9 7.6 collective-permute-done.185
  745.5 7.5 collective-permute-done.191
  756.4 6.2 collective-permute-done.197
  765.6 7.3 fusion.18
  773.0 7.1 fusion.20
  791.3 6.0 collective-permute-done.90
  800.3 7.2 collective-permute-done.96
  810.5 7.8 collective-permute-done.154
  821.3 7.0 collective-permute-done.160
  847.1 7.7 fusion.78
  856.3 6.0 fusion.123
  862.3 7.7 fusion.75
  870.7 6.0 fusion.111
  897.0 6.3 fusion.99
  1009.1 107.3 %collective-permute-done.254 = bf16[64,2048]{1,0:T(8,128)(2,1)S(1)} collective-permute-done((bf16[64,2048]{1,0:T(8,128)(2,1)S(1)}, bf16[64,2048]{1,0:T(8,128)(2,1)S(1)}, u32[]{:S(2)}, u32[]{:S(2)}) %collective-permute-start.254) | collective-permute-done | bytes 262176 | tf_op jit(solution)/shard_map/ppermute | solution.py:38
  1135.9 6.4 collective-permute-done.272
  1155.3 8.0 collective-permute-done.235
  1166.3 7.1 collective-permute-done.241
  1176.4 6.3 collective-permute-done.247
  1185.6 5.9 fusion.81
  1193.8 6.0 collective-permute-done.285
  1202.1 6.0 collective-permute-done.291
  1210.5 5.8 collective-permute-done.297
  1216.6 6.8 fusion.96
  1223.4 10.8 convert_bitcast_fusion
  1234.2 11.8 convert_bitcast_fusion.1
  1246.0 14.0 %convert_bitcast_fusion.2 = bf16[1,2048,2048]{2,1,0:T(8,128)(2,1)} fusion(bf16[1024,2048]{1,0:T(8,128)(2,1)} %get-tuple-element.2, bf16[256,2048]{1,0:T(8,128)(2,1)} %copy-done.9, bf16[256,2048]{1,0:T(8,128)(2,1)} %collective-permute-done.301, bf16[256,2048]{1,0:T(8,128)(2,1)S(1)} %collective-permute-done.300, bf16[256,2048]{1,0:T(8,128)(2,1)S(1)} %broadcast_multiply_fusion), kind=kOutput, calls=%fused_computation.51 | convolution fusion | flops 8610906112 | bytes 16777216 | tf_op jit(solution)/shard_map/dot_general | solution.py:70
  1260.0 6.7 add_convert_fusion.1
  1267.8 13.9 %pad_maximum_fusion = bf16[3,2048,2048]{2,1,0:T(8,128)(2,1)} fusion(bf16[1,2048,2048]{2,1,0:T(8,128)(2,1)S(1)} %convert_bitcast_fusion, bf16[1,2048,2048]{2,1,0:T(8,128)(2,1)S(1)} %convert_bitcast_fusion.1, bf16[1,2048,2048]{2,1,0:T(8,128)(2,1)} %convert_bitcast_fusion.2), kind=kLoop, calls=%fused_computation | loop fusion | flops 25165824 | bytes 50331648 | tf_op jit(solution)/shard_map/stack | solution.py:81
  1281.7 10.7 collective-permute-done.299
  (708 shorter events, 567.8 us)
Async XLA Ops:
  6.9 19.8 %collective-permute-start.42 = (bf16[64,2048]{1,0:T(8,128)(2,1)S(1)}, bf16[64,2048]{1,0:T(8,128)(2,1)S(1)}, u32[]{:S(2)}, u32[]{:S(2)}) collective-permute-start(bf16[64,2048]{1,0:T(8,128)(2,1)S(1)} %get-tuple-element.334), channel_id=1, source_target_pairs={{0,4},{1,5},{2,6},{3,7},{16,20},{17,21},{18,22},{19,23}} | collective-permute-start | bytes 786440 | tf_op jit(solution)/shard_map/ppermute | solution.py:38
  11.9 20.3 %collective-permute-start.45 = (bf16[64,2048]{1,0:T(8,128)(2,1)S(1)}, bf16[64,2048]{1,0:T(8,128)(2,1)S(1)}, u32[]{:S(2)}, u32[]{:S(2)}) collective-permute-start(bf16[64,2048]{1,0:T(8,128)(2,1)S(1)} %get-tuple-element.334), channel_id=1, source_target_pairs={{12,8},{13,9},{14,10},{15,11},{28,24},{29,25},{30,26},{31,27}} | collective-permute-start | bytes 786440 | tf_op jit(solution)/shard_map/ppermute | solution.py:38
  30.7 20.9 %collective-permute-start.18 = (bf16[64,2048]{1,0:T(8,128)(2,1)S(1)}, bf16[64,2048]{1,0:T(8,128)(2,1)S(1)}, u32[]{:S(2)}, u32[]{:S(2)}) collective-permute-start(bf16[64,2048]{1,0:T(8,128)(2,1)S(1)} %get-tuple-element.254), channel_id=1, source_target_pairs={{0,4},{1,5},{2,6},{3,7},{16,20},{17,21},{18,22},{19,23}} | collective-permute-start | bytes 786440 | tf_op jit(solution)/shard_map/ppermute | solution.py:38
  32.2 27.2 %collective-permute-start.21 = (bf16[64,2048]{1,0:T(8,128)(2,1)S(1)}, bf16[64,2048]{1,0:T(8,128)(2,1)S(1)}, u32[]{:S(2)}, u32[]{:S(2)}) collective-permute-start(bf16[64,2048]{1,0:T(8,128)(2,1)S(1)} %get-tuple-element.254), channel_id=1, source_target_pairs={{12,8},{13,9},{14,10},{15,11},{28,24},{29,25},{30,26},{31,27}} | collective-permute-start | bytes 786440 | tf_op jit(solution)/shard_map/ppermute | solution.py:38
  40.3 19.8 %collective-permute-start = (bf16[64,2048]{1,0:T(8,128)(2,1)S(1)}, bf16[64,2048]{1,0:T(8,128)(2,1)S(1)}, u32[]{:S(2)}, u32[]{:S(2)}) collective-permute-start(bf16[64,2048]{1,0:T(8,128)(2,1)S(1)} %get-tuple-element.257), channel_id=1, source_target_pairs={{0,4},{1,5},{2,6},{3,7},{16,20},{17,21},{18,22},{19,23}} | collective-permute-start | bytes 786440 | tf_op jit(solution)/shard_map/ppermute | solution.py:38
  59.4 19.7 %collective-permute-start.51 = (bf16[64,2048]{1,0:T(8,128)(2,1)S(1)}, bf16[64,2048]{1,0:T(8,128)(2,1)S(1)}, u32[]{:S(2)}, u32[]{:S(2)}) collective-permute-start(bf16[64,2048]{1,0:T(8,128)(2,1)S(1)} %get-tuple-element.177), channel_id=1, source_target_pairs={{12,8},{13,9},{14,10},{15,11},{28,24},{29,25},{30,26},{31,27}} | collective-permute-start | bytes 786440 | tf_op jit(solution)/shard_map/ppermute | solution.py:38
  60.1 19.7 %collective-permute-start.57 = (bf16[64,2048]{1,0:T(8,128)(2,1)S(1)}, bf16[64,2048]{1,0:T(8,128)(2,1)S(1)}, u32[]{:S(2)}, u32[]{:S(2)}) collective-permute-start(bf16[64,2048]{1,0:T(8,128)(2,1)S(1)} %get-tuple-element.176), channel_id=1, source_target_pairs={{12,8},{13,9},{14,10},{15,11},{28,24},{29,25},{30,26},{31,27}} | collective-permute-start | bytes 786440 | tf_op jit(solution)/shard_map/ppermute | solution.py:38
  99.6 26.1 %collective-permute-start.173 = (bf16[256,2048]{1,0:T(8,128)(2,1)S(1)}, bf16[256,2048]{1,0:T(8,128)(2,1)}, u32[]{:S(2)}, u32[]{:S(2)}) collective-permute-start(bf16[256,2048]{1,0:T(8,128)(2,1)S(1)} %get-tuple-element.100), channel_id=1, source_target_pairs={{0,2},{1,3},{2,0},{3,1},{4,6},{5,7},{6,4},{7,5},{8,10},{9,11},{10,... | collective-permute-start | bytes 3145736 | tf_op jit(solution)/shard_map/ppermute | solution.py:49
  108.6 24.5 %collective-permute-start.72 = (bf16[256,2048]{1,0:T(8,128)(2,1)S(1)}, bf16[256,2048]{1,0:T(8,128)(2,1)S(1)}, u32[]{:S(2)}, u32[]{:S(2)}) collective-permute-start(bf16[256,2048]{1,0:T(8,128)(2,1)S(1)} %get-tuple-element.99), channel_id=1, source_target_pairs={{0,1},{1,0},{2,3},{3,2},{4,5},{5,4},{6,7},{7,6},{8,9},{9,8},{10,11... | collective-permute-start | bytes 3145736 | tf_op jit(solution)/shard_map/ppermute | solution.py:50
  108.8 151.7 %collective-permute-start.148 = (bf16[256,2048]{1,0:T(8,128)(2,1)S(1)}, bf16[256,2048]{1,0:T(8,128)(2,1)}, u32[]{:S(2)}, u32[]{:S(2)}) collective-permute-start(bf16[256,2048]{1,0:T(8,128)(2,1)S(1)} %get-tuple-element.99), channel_id=1, source_target_pairs={{0,2},{1,3},{2,0},{3,1},{4,6},{5,7},{6,4},{7,5},{8,10},{9,11},{10,... | collective-permute-start | bytes 3145736 | tf_op jit(solution)/shard_map/ppermute | solution.py:49
  109.3 184.0 %collective-permute-start.122 = (bf16[256,2048]{1,0:T(8,128)(2,1)S(1)}, bf16[256,2048]{1,0:T(8,128)(2,1)S(1)}, u32[]{:S(2)}, u32[]{:S(2)}) collective-permute-start(bf16[256,2048]{1,0:T(8,128)(2,1)S(1)} %get-tuple-element.98), channel_id=1, source_target_pairs={{0,1},{1,0},{2,3},{3,2},{4,5},{5,4},{6,7},{7,6},{8,9},{9,8},{10,11... | collective-permute-start | bytes 3145736 | tf_op jit(solution)/shard_map/ppermute | solution.py:50
  109.7 212.1 %collective-permute-start.198 = (bf16[256,2048]{1,0:T(8,128)(2,1)S(1)}, bf16[256,2048]{1,0:T(8,128)(2,1)S(1)}, u32[]{:S(2)}, u32[]{:S(2)}) collective-permute-start(bf16[256,2048]{1,0:T(8,128)(2,1)S(1)} %get-tuple-element.98), channel_id=1, source_target_pairs={{0,2},{1,3},{2,0},{3,1},{4,6},{5,7},{6,4},{7,5},{8,10},{9,11},{10,... | collective-permute-start | bytes 3145736 | tf_op jit(solution)/shard_map/ppermute | solution.py:49
  125.7 92.4 %collective-permute-start.29 = (bf16[64,2048]{1,0:T(8,128)(2,1)S(1)}, bf16[64,2048]{1,0:T(8,128)(2,1)S(1)}, u32[]{:S(2)}, u32[]{:S(2)}) collective-permute-start(bf16[64,2048]{1,0:T(8,128)(2,1)S(1)} %get-tuple-element.323), channel_id=1, source_target_pairs={{4,0},{5,1},{6,2},{7,3},{20,16},{21,17},{22,18},{23,19}} | collective-permute-start | bytes 786440 | tf_op jit(solution)/shard_map/ppermute | solution.py:38
  133.0 86.3 %collective-permute-start.26 = (bf16[64,2048]{1,0:T(8,128)(2,1)S(1)}, bf16[64,2048]{1,0:T(8,128)(2,1)S(1)}, u32[]{:S(2)}, u32[]{:S(2)}) collective-permute-start(bf16[64,2048]{1,0:T(8,128)(2,1)S(1)} %get-tuple-element.339), channel_id=1, source_target_pairs={{8,12},{9,13},{10,14},{11,15},{24,28},{25,29},{26,30},{27,31}} | collective-permute-start | bytes 786440 | tf_op jit(solution)/shard_map/ppermute | solution.py:38
  279.0 20.8 %collective-permute-start.53 = (bf16[64,2048]{1,0:T(8,128)(2,1)S(1)}, bf16[64,2048]{1,0:T(8,128)(2,1)S(1)}, u32[]{:S(2)}, u32[]{:S(2)}) collective-permute-start(bf16[64,2048]{1,0:T(8,128)(2,1)S(1)} %get-tuple-element.163), channel_id=1, source_target_pairs={{4,0},{5,1},{6,2},{7,3},{20,16},{21,17},{22,18},{23,19}} | collective-permute-start | bytes 786440 | tf_op jit(solution)/shard_map/ppermute | solution.py:38
  285.2 20.0 %collective-permute-start.65 = (bf16[64,2048]{1,0:T(8,128)(2,1)S(1)}, bf16[64,2048]{1,0:T(8,128)(2,1)S(1)}, u32[]{:S(2)}, u32[]{:S(2)}) collective-permute-start(bf16[64,2048]{1,0:T(8,128)(2,1)S(1)} %get-tuple-element.167), channel_id=1, source_target_pairs={{4,0},{5,1},{6,2},{7,3},{20,16},{21,17},{22,18},{23,19}} | collective-permute-start | bytes 786440 | tf_op jit(solution)/shard_map/ppermute | solution.py:38
  305.3 23.1 %collective-permute-start.116 = (bf16[64,2048]{1,0:T(8,128)(2,1)S(1)}, bf16[64,2048]{1,0:T(8,128)(2,1)S(1)}, u32[]{:S(2)}, u32[]{:S(2)}) collective-permute-start(bf16[64,2048]{1,0:T(8,128)(2,1)S(1)} %get-tuple-element.314), channel_id=1, source_target_pairs={{0,4},{1,5},{2,6},{3,7},{16,20},{17,21},{18,22},{19,23}} | collective-permute-start | bytes 786440 | tf_op jit(solution)/shard_map/ppermute | solution.py:38
  309.9 23.2 %collective-permute-start.119 = (bf16[64,2048]{1,0:T(8,128)(2,1)S(1)}, bf16[64,2048]{1,0:T(8,128)(2,1)S(1)}, u32[]{:S(2)}, u32[]{:S(2)}) collective-permute-start(bf16[64,2048]{1,0:T(8,128)(2,1)S(1)} %get-tuple-element.314), channel_id=1, source_target_pairs={{12,8},{13,9},{14,10},{15,11},{28,24},{29,25},{30,26},{31,27}} | collective-permute-start | bytes 786440 | tf_op jit(solution)/shard_map/ppermute | solution.py:38
  312.2 21.6 %collective-permute-start.98 = (bf16[64,2048]{1,0:T(8,128)(2,1)S(1)}, bf16[64,2048]{1,0:T(8,128)(2,1)S(1)}, u32[]{:S(2)}, u32[]{:S(2)}) collective-permute-start(bf16[64,2048]{1,0:T(8,128)(2,1)S(1)} %get-tuple-element.317), channel_id=1, source_target_pairs={{0,4},{1,5},{2,6},{3,7},{16,20},{17,21},{18,22},{19,23}} | collective-permute-start | bytes 786440 | tf_op jit(solution)/shard_map/ppermute | solution.py:38
  350.0 20.9 %collective-permute-start.91 = (bf16[64,2048]{1,0:T(8,128)(2,1)S(1)}, bf16[64,2048]{1,0:T(8,128)(2,1)S(1)}, u32[]{:S(2)}, u32[]{:S(2)}) collective-permute-start(bf16[64,2048]{1,0:T(8,128)(2,1)S(1)} %get-tuple-element.234), channel_id=1, source_target_pairs={{0,4},{1,5},{2,6},{3,7},{16,20},{17,21},{18,22},{19,23}} | collective-permute-start | bytes 786440 | tf_op jit(solution)/shard_map/ppermute | solution.py:38
  351.4 24.0 %collective-permute-start.76 = (bf16[64,2048]{1,0:T(8,128)(2,1)S(1)}, bf16[64,2048]{1,0:T(8,128)(2,1)S(1)}, u32[]{:S(2)}, u32[]{:S(2)}) collective-permute-start(bf16[64,2048]{1,0:T(8,128)(2,1)S(1)} %get-tuple-element.237), channel_id=1, source_target_pairs={{12,8},{13,9},{14,10},{15,11},{28,24},{29,25},{30,26},{31,27}} | collective-permute-start | bytes 786440 | tf_op jit(solution)/shard_map/ppermute | solution.py:38
  354.1 24.7 %collective-permute-start.94 = (bf16[64,2048]{1,0:T(8,128)(2,1)S(1)}, bf16[64,2048]{1,0:T(8,128)(2,1)S(1)}, u32[]{:S(2)}, u32[]{:S(2)}) collective-permute-start(bf16[64,2048]{1,0:T(8,128)(2,1)S(1)} %get-tuple-element.234), channel_id=1, source_target_pairs={{12,8},{13,9},{14,10},{15,11},{28,24},{29,25},{30,26},{31,27}} | collective-permute-start | bytes 786440 | tf_op jit(solution)/shard_map/ppermute | solution.py:38
  359.7 19.8 %collective-permute-start.73 = (bf16[64,2048]{1,0:T(8,128)(2,1)S(1)}, bf16[64,2048]{1,0:T(8,128)(2,1)S(1)}, u32[]{:S(2)}, u32[]{:S(2)}) collective-permute-start(bf16[64,2048]{1,0:T(8,128)(2,1)S(1)} %get-tuple-element.237), channel_id=1, source_target_pairs={{0,4},{1,5},{2,6},{3,7},{16,20},{17,21},{18,22},{19,23}} | collective-permute-start | bytes 786440 | tf_op jit(solution)/shard_map/ppermute | solution.py:38
  395.8 20.7 %collective-permute-start.141 = (bf16[64,2048]{1,0:T(8,128)(2,1)S(1)}, bf16[64,2048]{1,0:T(8,128)(2,1)S(1)}, u32[]{:S(2)}, u32[]{:S(2)}) collective-permute-start(bf16[64,2048]{1,0:T(8,128)(2,1)S(1)} %get-tuple-element.154), channel_id=1, source_target_pairs={{0,4},{1,5},{2,6},{3,7},{16,20},{17,21},{18,22},{19,23}} | collective-permute-start | bytes 786440 | tf_op jit(solution)/shard_map/ppermute | solution.py:38
  397.6 27.1 %collective-permute-start.144 = (bf16[64,2048]{1,0:T(8,128)(2,1)S(1)}, bf16[64,2048]{1,0:T(8,128)(2,1)S(1)}, u32[]{:S(2)}, u32[]{:S(2)}) collective-permute-start(bf16[64,2048]{1,0:T(8,128)(2,1)S(1)} %get-tuple-element.154), channel_id=1, source_target_pairs={{12,8},{13,9},{14,10},{15,11},{28,24},{29,25},{30,26},{31,27}} | collective-permute-start | bytes 786440 | tf_op jit(solution)/shard_map/ppermute | solution.py:38
  405.3 20.1 %collective-permute-start.123 = (bf16[64,2048]{1,0:T(8,128)(2,1)S(1)}, bf16[64,2048]{1,0:T(8,128)(2,1)S(1)}, u32[]{:S(2)}, u32[]{:S(2)}) collective-permute-start(bf16[64,2048]{1,0:T(8,128)(2,1)S(1)} %get-tuple-element.157), channel_id=1, source_target_pairs={{0,4},{1,5},{2,6},{3,7},{16,20},{17,21},{18,22},{19,23}} | collective-permute-start | bytes 786440 | tf_op jit(solution)/shard_map/ppermute | solution.py:38
  472.0 450.0 %collective-permute-start.301 = (bf16[256,2048]{1,0:T(8,128)(2,1)S(1)}, bf16[256,2048]{1,0:T(8,128)(2,1)}, u32[]{:S(2)}, u32[]{:S(2)}) collective-permute-start(bf16[256,2048]{1,0:T(8,128)(2,1)S(1)} %broadcast_multiply_fusion), channel_id=1, source_target_pairs={{0,2},{1,3},{2,0},{3,1},{4,6},{5,7},{6,4},{7,5},{8,10},{9,11},{10,... | collective-permute-start | bytes 3145736 | tf_op jit(solution)/shard_map/ppermute | solution.py:49
  473.1 381.7 %collective-permute-start.248 = (bf16[256,2048]{1,0:T(8,128)(2,1)}, bf16[256,2048]{1,0:T(8,128)(2,1)}, u32[]{:S(2)}, u32[]{:S(2)}) collective-permute-start(bf16[256,2048]{1,0:T(8,128)(2,1)} %collective-permute-done.173), channel_id=1, source_target_pairs={{0,1},{1,0},{2,3},{3,2},{4,5},{5,4},{6,7},{7,6},{8,9},{9,8},{10,11... | collective-permute-start | bytes 3145736 | tf_op jit(solution)/shard_map/ppermute | solution.py:50
  487.6 382.4 %collective-permute-start.223 = (bf16[256,2048]{1,0:T(8,128)(2,1)}, bf16[256,2048]{1,0:T(8,128)(2,1)}, u32[]{:S(2)}, u32[]{:S(2)}) collective-permute-start(bf16[256,2048]{1,0:T(8,128)(2,1)} %collective-permute-done.148), channel_id=1, source_target_pairs={{0,1},{1,0},{2,3},{3,2},{4,5},{5,4},{6,7},{7,6},{8,9},{9,8},{10,11... | collective-permute-start | bytes 3145736 | tf_op jit(solution)/shard_map/ppermute | solution.py:50
  488.2 209.1 %collective-permute-start.103 = (bf16[64,2048]{1,0:T(8,128)(2,1)S(1)}, bf16[64,2048]{1,0:T(8,128)(2,1)S(1)}, u32[]{:S(2)}, u32[]{:S(2)}) collective-permute-start(bf16[64,2048]{1,0:T(8,128)(2,1)S(1)} %get-tuple-element.303), channel_id=1, source_target_pairs={{4,0},{5,1},{6,2},{7,3},{20,16},{21,17},{22,18},{23,19}} | collective-permute-start | bytes 786440 | tf_op jit(solution)/shard_map/ppermute | solution.py:38
  489.5 209.1 %collective-permute-start.100 = (bf16[64,2048]{1,0:T(8,128)(2,1)S(1)}, bf16[64,2048]{1,0:T(8,128)(2,1)S(1)}, u32[]{:S(2)}, u32[]{:S(2)}) collective-permute-start(bf16[64,2048]{1,0:T(8,128)(2,1)S(1)} %get-tuple-element.319), channel_id=1, source_target_pairs={{8,12},{9,13},{10,14},{11,15},{24,28},{25,29},{26,30},{27,31}} | collective-permute-start | bytes 786440 | tf_op jit(solution)/shard_map/ppermute | solution.py:38
  844.8 58.6 %collective-permute-start.273 = (bf16[256,2048]{1,0:T(8,128)(2,1)S(1)}, bf16[256,2048]{1,0:T(8,128)(2,1)S(1)}, u32[]{:S(2)}, u32[]{:S(2)}) collective-permute-start(bf16[256,2048]{1,0:T(8,128)(2,1)S(1)} %copy-done.8), channel_id=1, source_target_pairs={{0,1},{1,0},{2,3},{3,2},{4,5},{5,4},{6,7},{7,6},{8,9},{9,8},{10,11... | collective-permute-start | bytes 3145736 | tf_op jit(solution)/shard_map/ppermute | solution.py:50
  844.8 31.9 %collective-permute-start.128 = (bf16[64,2048]{1,0:T(8,128)(2,1)S(1)}, bf16[64,2048]{1,0:T(8,128)(2,1)S(1)}, u32[]{:S(2)}, u32[]{:S(2)}) collective-permute-start(bf16[64,2048]{1,0:T(8,128)(2,1)S(1)} %get-tuple-element.143), channel_id=1, source_target_pairs={{4,0},{5,1},{6,2},{7,3},{20,16},{21,17},{22,18},{23,19}} | collective-permute-start | bytes 786440 | tf_op jit(solution)/shard_map/ppermute | solution.py:38
  854.8 24.9 %collective-permute-start.134 = (bf16[64,2048]{1,0:T(8,128)(2,1)S(1)}, bf16[64,2048]{1,0:T(8,128)(2,1)S(1)}, u32[]{:S(2)}, u32[]{:S(2)}) collective-permute-start(bf16[64,2048]{1,0:T(8,128)(2,1)S(1)} %get-tuple-element.145), channel_id=1, source_target_pairs={{4,0},{5,1},{6,2},{7,3},{20,16},{21,17},{22,18},{23,19}} | collective-permute-start | bytes 786440 | tf_op jit(solution)/shard_map/ppermute | solution.py:38
  888.5 21.4 %collective-permute-start.204 = (bf16[64,2048]{1,0:T(8,128)(2,1)S(1)}, bf16[64,2048]{1,0:T(8,128)(2,1)S(1)}, u32[]{:S(2)}, u32[]{:S(2)}) collective-permute-start(bf16[64,2048]{1,0:T(8,128)(2,1)S(1)} %get-tuple-element.123), channel_id=1, source_target_pairs={{4,0},{5,1},{6,2},{7,3},{20,16},{21,17},{22,18},{23,19}} | collective-permute-start | bytes 786440 | tf_op jit(solution)/shard_map/ppermute | solution.py:38
  894.7 20.6 %collective-permute-start.216 = (bf16[64,2048]{1,0:T(8,128)(2,1)S(1)}, bf16[64,2048]{1,0:T(8,128)(2,1)S(1)}, u32[]{:S(2)}, u32[]{:S(2)}) collective-permute-start(bf16[64,2048]{1,0:T(8,128)(2,1)S(1)} %get-tuple-element.127), channel_id=1, source_target_pairs={{4,0},{5,1},{6,2},{7,3},{20,16},{21,17},{22,18},{23,19}} | collective-permute-start | bytes 786440 | tf_op jit(solution)/shard_map/ppermute | solution.py:38
  931.7 20.9 %collective-permute-start.242 = (bf16[64,2048]{1,0:T(8,128)(2,1)S(1)}, bf16[64,2048]{1,0:T(8,128)(2,1)S(1)}, u32[]{:S(2)}, u32[]{:S(2)}) collective-permute-start(bf16[64,2048]{1,0:T(8,128)(2,1)S(1)} %get-tuple-element.194), channel_id=1, source_target_pairs={{0,4},{1,5},{2,6},{3,7},{16,20},{17,21},{18,22},{19,23}} | collective-permute-start | bytes 786440 | tf_op jit(solution)/shard_map/ppermute | solution.py:38
  934.0 26.4 %collective-permute-start.245 = (bf16[64,2048]{1,0:T(8,128)(2,1)S(1)}, bf16[64,2048]{1,0:T(8,128)(2,1)S(1)}, u32[]{:S(2)}, u32[]{:S(2)}) collective-permute-start(bf16[64,2048]{1,0:T(8,128)(2,1)S(1)} %get-tuple-element.194), channel_id=1, source_target_pairs={{12,8},{13,9},{14,10},{15,11},{28,24},{29,25},{30,26},{31,27}} | collective-permute-start | bytes 786440 | tf_op jit(solution)/shard_map/ppermute | solution.py:38
  941.4 19.8 %collective-permute-start.224 = (bf16[64,2048]{1,0:T(8,128)(2,1)S(1)}, bf16[64,2048]{1,0:T(8,128)(2,1)S(1)}, u32[]{:S(2)}, u32[]{:S(2)}) collective-permute-start(bf16[64,2048]{1,0:T(8,128)(2,1)S(1)} %get-tuple-element.197), channel_id=1, source_target_pairs={{0,4},{1,5},{2,6},{3,7},{16,20},{17,21},{18,22},{19,23}} | collective-permute-start | bytes 786440 | tf_op jit(solution)/shard_map/ppermute | solution.py:38
  960.5 19.7 %collective-permute-start.277 = (bf16[64,2048]{1,0:T(8,128)(2,1)S(1)}, bf16[64,2048]{1,0:T(8,128)(2,1)S(1)}, u32[]{:S(2)}, u32[]{:S(2)}) collective-permute-start(bf16[64,2048]{1,0:T(8,128)(2,1)S(1)} %get-tuple-element.117), channel_id=1, source_target_pairs={{12,8},{13,9},{14,10},{15,11},{28,24},{29,25},{30,26},{31,27}} | collective-permute-start | bytes 786440 | tf_op jit(solution)/shard_map/ppermute | solution.py:38
  961.2 19.7 %collective-permute-start.283 = (bf16[64,2048]{1,0:T(8,128)(2,1)S(1)}, bf16[64,2048]{1,0:T(8,128)(2,1)S(1)}, u32[]{:S(2)}, u32[]{:S(2)}) collective-permute-start(bf16[64,2048]{1,0:T(8,128)(2,1)S(1)} %get-tuple-element.116), channel_id=1, source_target_pairs={{12,8},{13,9},{14,10},{15,11},{28,24},{29,25},{30,26},{31,27}} | collective-permute-start | bytes 786440 | tf_op jit(solution)/shard_map/ppermute | solution.py:38
  998.6 224.7 %collective-permute-start.300 = (bf16[256,2048]{1,0:T(8,128)(2,1)S(1)}, bf16[256,2048]{1,0:T(8,128)(2,1)S(1)}, u32[]{:S(2)}, u32[]{:S(2)}) collective-permute-start(bf16[256,2048]{1,0:T(8,128)(2,1)S(1)} %broadcast_multiply_fusion), channel_id=1, source_target_pairs={{0,1},{1,0},{2,3},{3,2},{4,5},{5,4},{6,7},{7,6},{8,9},{9,8},{10,11... | collective-permute-start | bytes 3145736 | tf_op jit(solution)/shard_map/ppermute | solution.py:50
  998.7 224.7 %collective-permute-start.302 = (bf16[256,2048]{1,0:T(8,128)(2,1)}, bf16[256,2048]{1,0:T(8,128)(2,1)S(1)}, u32[]{:S(2)}, u32[]{:S(2)}) collective-permute-start(bf16[256,2048]{1,0:T(8,128)(2,1)} %collective-permute-done.301), channel_id=1, source_target_pairs={{0,1},{1,0},{2,3},{3,2},{4,5},{5,4},{6,7},{7,6},{8,9},{9,8},{10,11... | collective-permute-start | bytes 3145736 | tf_op jit(solution)/shard_map/ppermute | solution.py:50
  1006.7 275.0 %collective-permute-start.147 = (bf16[256,2048]{1,0:T(8,128)(2,1)S(1)}, bf16[256,2048]{1,0:T(8,128)(2,1)S(1)}, u32[]{:S(2)}, u32[]{:S(2)}) collective-permute-start(bf16[256,2048]{1,0:T(8,128)(2,1)S(1)} %fusion.99), channel_id=1, source_target_pairs={{0,1},{1,0},{2,3},{3,2},{4,5},{5,4},{6,7},{7,6},{8,9},{9,8},{10,11... | collective-permute-start | bytes 3145736 | tf_op jit(solution)/shard_map/ppermute | solution.py:79
  1006.8 109.6 %collective-permute-start.254 = (bf16[64,2048]{1,0:T(8,128)(2,1)S(1)}, bf16[64,2048]{1,0:T(8,128)(2,1)S(1)}, u32[]{:S(2)}, u32[]{:S(2)}) collective-permute-start(bf16[64,2048]{1,0:T(8,128)(2,1)S(1)} %get-tuple-element.263), channel_id=1, source_target_pairs={{4,0},{5,1},{6,2},{7,3},{20,16},{21,17},{22,18},{23,19}} | collective-permute-start | bytes 786440 | tf_op jit(solution)/shard_map/ppermute | solution.py:38
  1008.1 109.6 %collective-permute-start.251 = (bf16[64,2048]{1,0:T(8,128)(2,1)S(1)}, bf16[64,2048]{1,0:T(8,128)(2,1)S(1)}, u32[]{:S(2)}, u32[]{:S(2)}) collective-permute-start(bf16[64,2048]{1,0:T(8,128)(2,1)S(1)} %get-tuple-element.279), channel_id=1, source_target_pairs={{8,12},{9,13},{10,14},{11,15},{24,28},{25,29},{26,30},{27,31}} | collective-permute-start | bytes 786440 | tf_op jit(solution)/shard_map/ppermute | solution.py:38
  1223.4 36.6 %collective-permute-start.298 = (bf16[256,2048]{1,0:T(8,128)(2,1)}, bf16[256,2048]{1,0:T(8,128)(2,1)}, u32[]{:S(2)}, u32[]{:S(2)}) collective-permute-start(bf16[256,2048]{1,0:T(8,128)(2,1)} %fusion.96), channel_id=1, source_target_pairs={{0,1},{1,0},{2,3},{3,2},{4,5},{5,4},{6,7},{7,6},{8,9},{9,8},{10,11... | collective-permute-start | bytes 3145736 | tf_op jit(solution)/shard_map/ppermute | solution.py:77
  1266.7 25.6 %collective-permute-start.299 = (bf16[256,2048]{1,0:T(8,128)(2,1)S(1)}, bf16[256,2048]{1,0:T(8,128)(2,1)S(1)}, u32[]{:S(2)}, u32[]{:S(2)}) collective-permute-start(bf16[256,2048]{1,0:T(8,128)(2,1)S(1)} %add_convert_fusion.1), channel_id=1, source_target_pairs={{0,2},{1,3},{2,0},{3,1},{4,6},{5,7},{6,4},{7,5},{8,10},{9,11},{10,... | collective-permute-start | bytes 3145736 | tf_op jit(solution)/shard_map/ppermute | solution.py:78
  (266 other events, 2210.0 us)
